TPU v7x, 32 devices: a whole 2x2x4 slice. The times are simulated.
32 devices in a mesh: task: 4 (over z), unit: 8 (over y, x, core).
Axes of the slice: x: 2, y: 2, z: 4, core: 2. Of those that a mesh axis runs over, the one named last changes fastest.
Arguments:
- tokens: bfloat16 [64, 4096], P(('task', 'unit')), may hold values from -6 to 6
- router: float32 [64, 4], P('unit', 'task'), may hold values from 0.1 to 1
- base_gate: bfloat16 [16384, 4096], P(('task', 'unit')), may hold values from -0.09375 to 0.09375
- base_up: bfloat16 [16384, 4096], P(('task', 'unit')), may hold values from -0.09375 to 0.09375
- base_down: bfloat16 [16384, 4096], P(('task', 'unit')), may hold values from -0.046875 to 0.046875
- task_gate: bfloat16 [4, 16384, 4096], P('task', 'unit'), may hold values from -0.09375 to 0.09375
- task_up: bfloat16 [4, 16384, 4096], P('task', 'unit'), may hold values from -0.09375 to 0.09375
- task_down: bfloat16 [4, 16384, 4096], P('task', 'unit'), may hold values from -0.046875 to 0.046875
Outputs:
- mixed: bfloat16 [64, 4096], P(('task', 'unit'))
All inputs are finite; a program needn't handle non-finite values.
Results may differ from a plain program's by a relative error of at most 0.0049.
Values may be sent and summed in bfloat16 or wider, within the bound.
A program may use at most 128 MiB of HBM per device.

v0:
```python
import jax
import jax.numpy as jnp
from jax import lax
from jax.sharding import PartitionSpec as P


def project_rows(rows, weight):
    dims = (((1,), (1,)), ((), ()))
    return lax.dot_general(rows, weight, dims, preferred_element_type=jnp.float32)


def body(tokens, router, base_gate, base_up, base_down, task_gate, task_up, task_down):
    weights_all = lax.all_gather(router, "unit", axis=0, tiled=True)
    own_gate = task_gate[0]
    own_up = task_up[0]
    own_down = task_down[0]
    base_width = base_gate.shape[0]
    piece = lax.all_gather(tokens, ("task", "unit"), axis=0, tiled=True)
    base_part = jax.nn.silu(project_rows(piece, base_gate)) * project_rows(piece, base_up)
    task_part = (
        jax.nn.silu(project_rows(piece, own_gate)) * project_rows(piece, own_up) * weights_all
    )
    hidden = jnp.concatenate([base_part.astype(jnp.bfloat16), task_part.astype(jnp.bfloat16)], 1)
    base_term = jnp.dot(hidden[:, :base_width], base_down, preferred_element_type=jnp.float32)
    task_term = jnp.dot(hidden[:, base_width:], own_down, preferred_element_type=jnp.float32)
    summed = lax.psum_scatter(
        base_term + task_term, ("task", "unit"), scatter_dimension=0, tiled=True
    )
    return summed.astype(jnp.bfloat16)


def solution(mesh):
    in_specs = (
        P(("task", "unit"), None),
        P("unit", "task"),
        P(("task", "unit"), None),
        P(("task", "unit"), None),
        P(("task", "unit"), None),
        P("task", "unit", None),
        P("task", "unit", None),
        P("task", "unit", None),
    )
    out_specs = P(("task", "unit"), None)
    return jax.shard_map(body, mesh=mesh, in_specs=in_specs, out_specs=out_specs, check_vma=False)
```

profile of v0, /device:TPU:0, one launch (start us, length us, event | category | flops | bytes accessed | tf_op | source)
XLA Modules:
  0.0 142.7 jit_solution(15645531527904311101)
XLA Ops:
  0.0 0.0 copy-start.1
  0.0 0.0 copy-start
  0.0 45.0 %all-gather = bf16[32,2,4096]{2,1,0:T(2,128)(2,1)S(1)} all-gather(bf16[1,2,4096]{2,1,0:T(2,128)(2,1)} %bitcast.28), channel_id=1, replica_groups=mesh['task'=4,'unit'=8] {'task','unit'}, dimensions={0}, use_global_device_ids=true | all-gather | bytes 540672 | tf_op jit(solution)/shard_map/all_gather | solution.py:18
  45.0 0.2 reshape.4
  45.2 11.0 %fusion.4 = f32[64,2048]{1,0:T(8,128)S(1)} fusion(bf16[64,4096]{1,0:T(8,128)(2,1)S(1)} %reshape.4, bf16[1,2048,4096]{2,1,0:T(8,128)(2,1)} %param.13), kind=kOutput, calls=%fused_computation.4 | convolution fusion | flops 1073741824 | bytes 17825792 | tf_op jit(solution)/shard_map/dot_general | solution.py:9
  56.2 0.0 copy-done.1
  56.2 0.6 dynamic-slice
  57.4 0.0 copy-done
  57.4 0.1 bitcast_dynamic-update-slice_fusion
  57.5 12.1 %all-reduce = f32[64]{0:T(128)S(1)} all-reduce(f32[64]{0:T(128)S(1)} %bitcast_dynamic-update-slice_fusion), channel_id=1, replica_groups=mesh['task'=4,'unit'=8] {'unit'}, use_global_device_ids=true, to_apply=%add | all-reduce | flops 64 | bytes 512
  69.6 14.7 %fusion = f32[64,4096]{1,0:T(8,128)S(1)} fusion(bf16[1,2048,4096]{2,1,0:T(8,128)(2,1)} %param.15, bf16[64,4096]{1,0:T(8,128)(2,1)S(1)} %reshape.4, bf16[1,2048,4096]{2,1,0:T(8,128)(2,1)} %param.14, f32[64,2048]{1,0:T(8,128)S(1)} %fusion.4, f32[64]{0:T(128)S(1)} %all-reduce), kind=kOutput, calls=%fused_computation | convolution fusion | flops 2148401152 | bytes 35651840 | tf_op jit(solution)/shard_map/dot_general | solution.py:25
  84.4 3.6 %fusion.33 = f32[64,512]{1,0:T(8,128)S(1)} fusion(bf16[64,4096]{1,0:T(8,128)(2,1)S(1)} %reshape.4, bf16[512,4096]{1,0:T(8,128)(2,1)} %param.10), kind=kOutput, calls=%fused_computation.29 | convolution fusion | flops 268435456 | bytes 4849664 | tf_op jit(solution)/shard_map/dot_general | solution.py:9
  87.9 5.7 %convolution_add_fusion = f32[64,4096]{1,0:T(8,128)S(1)} fusion(f32[64,4096]{1,0:T(8,128)S(1)} %fusion, bf16[512,4096]{1,0:T(8,128)(2,1)} %param.12, bf16[64,4096]{1,0:T(8,128)(2,1)S(1)} %reshape.4, bf16[512,4096]{1,0:T(8,128)(2,1)} %param.11, f32[64,512]{1,0:T(8,128)S(1)} %fusion.33), kind=kOutput, calls=%fused_computation.6 | convolution fusion | flops 537329664 | bytes 11141120 | tf_op jit(solution)/shard_map/dot_general | solution.py:24
  93.6 48.4 %all-reduce.3 = bf16[64,4096]{1,0:T(8,128)(2,1)S(1)} all-reduce(f32[64,4096]{1,0:T(8,128)S(1)} %convolution_add_fusion), channel_id=2, replica_groups=mesh['task'=4,'unit'=8] {'task','unit'}, use_global_device_ids=true, to_apply=%region_0.1.clone | all-reduce | flops 262144 | bytes 1572864
  142.0 0.6 dynamic-slice_convert_fusion
  (1 shorter events, 0.0 us)
Async XLA Ops:
  0.0 56.2 %copy-start.1 = (u32[32]{0:T(128)S(1)}, u32[32]{0:T(128)}, u32[]{:S(2)}) copy-start(u32[32]{0:T(128)} %constant.12) | copy-start | bytes 388
  0.0 57.4 %copy-start = (f32[8,1]{0,1:T(1,128)S(1)}, f32[8,1]{0,1:T(1,128)}, u32[]{:S(2)}) copy-start(f32[8,1]{0,1:T(1,128)} %param.9) | copy-start | bytes 100
where the time goes:
time: 143 us
  blocking collectives  106 us (74%)
  matrix products  34.9 us (24%)
  local copies, waits for them, and re-layouts  1.52 us (1%)
    unnamed x2, blocking collectives  60.5 us
    all_gather x1, blocking collectives, body(): piece = lax.all_gather(tokens, ('task', 'unit'), axis=0, tiled=True)  45 us
    dot_general x1, matrix products, body(): jnp.dot(hidden[:, base_width:], own_down, preferred_element_type=jnp.floa...  14.7 us
    dot_general x2, matrix products, project_rows(): lax.dot_general(rows, weight, dims, preferred_element_type=jnp.float32)  14.5 us
    dot_general x1, matrix products, body(): jnp.dot(hidden[:, :base_width], base_down, preferred_element_type=jnp.flo...  5.67 us

commit v1 on v0

v1 whole, which is shorter than its diff:
```python
import functools
import math

import jax
import jax.numpy as jnp
from jax import lax
from jax.experimental import pallas as pl
from jax.experimental.pallas import tpu as pltpu
from jax.sharding import PartitionSpec as P

MESH = pl.DeviceIdType.MESH
F32 = jnp.float32
BF16 = jnp.bfloat16
COLS = 512
REUSE = 1


def kernel(
    n_task, n_unit, tok_ref, router_ref, bg, bu, bd, tg, tu, td, out_ref,
    gate_v, up_v, down_v, hid, x_v, tokbuf, g1, rows8, wbuf, wcol,
    part, send_a, recv_a, send_b, recv_b, send_c, recv_c, own_c,
    gsem, usem, dsem, g1s, g1r, g2s, g2r, g3s, g3r, ws, wr,
    as_, ar, bs, br, cs, cr,
):
    t = lax.axis_index("task")
    u = lax.axis_index("unit")
    n_xy = n_unit // 2
    c = lax.rem(u, 2)
    xy = u // 2
    rows, d_model = tok_ref.shape
    group = n_task * rows
    tokens = group * n_unit
    half = tokens // 2
    base_w, task_w = bg.shape[0], tg.shape[1]
    n_hid, _, unit_w = hid.shape
    n_base = base_w // unit_w
    n_col = d_model // COLS
    kept = n_col - REUSE

    for i in range(n_hid):
        for base, task, buf, sem in ((bg, tg, gate_v, gsem), (bu, tu, up_v, usem)):
            if i < n_base:
                src = base.at[pl.ds(i * unit_w, unit_w)]
            else:
                src = task.at[0, pl.ds((i - n_base) * unit_w, unit_w)]
            pltpu.make_async_copy(src, buf.at[pl.ds(i * unit_w, unit_w)], sem.at[i]).start()

    def down_copies(j):
        cols = pl.ds(j * COLS, COLS)
        if j < kept:
            lo, hi = down_v.at[j, pl.ds(0, base_w)], down_v.at[j, pl.ds(base_w, task_w)]
        else:
            spot = pl.ds((j - kept) * COLS, COLS)
            lo, hi = gate_v.at[pl.ds(0, base_w), spot], gate_v.at[pl.ds(base_w, task_w), spot]
        return (
            pltpu.make_async_copy(bd.at[:, cols], lo, dsem.at[j, 0]),
            pltpu.make_async_copy(td.at[0, :, cols], hi, dsem.at[j, 1]),
        )

    for j in range(kept):
        for copy in down_copies(j):
            copy.start()

    barrier = pltpu.get_barrier_semaphore()
    for d in range(1, n_task):
        pl.semaphore_signal(barrier, inc=1, device_id=(lax.rem(t + d, n_task), u), device_id_type=MESH)
    for d in range(1, n_unit):
        pl.semaphore_signal(barrier, inc=1, device_id=(t, lax.rem(u + d, n_unit)), device_id_type=MESH)
    pl.semaphore_wait(barrier, n_task + n_unit - 2)

    def remote(src, dst, ssem, rsem, dev):
        return pltpu.make_async_remote_copy(
            src_ref=src, dst_ref=dst, send_sem=ssem, recv_sem=rsem, device_id=dev, device_id_type=MESH
        )

    sibling = (t, xy * 2 + 1 - c)

    def peer_xy(d):
        return lax.rem(xy + d, n_xy)

    first = [
        remote(tok_ref, g1.at[t], g1s.at[d], g1r.at[d], (lax.rem(t + d, n_task), u))
        for d in range(1, n_task)
    ]
    for copy in first:
        copy.start()
    weights = [
        remote(router_ref, wbuf.at[u], ws.at[d], wr.at[d], (t, lax.rem(u + d, n_unit)))
        for d in range(1, n_unit)
    ]
    for copy in weights:
        copy.start()
    g1[t] = tok_ref[...]
    wbuf[u] = router_ref[...]
    for copy in first:
        copy.wait()
    for s in range(n_task):
        rows8[pl.ds(s * rows, rows), :] = g1[s].astype(F32)
    whole = rows8[...]
    mid = d_model // 2
    tokbuf[c, xy] = jnp.concatenate([whole[:, :mid], whole[:, mid:]], 0).astype(BF16)
    second = [
        remote(tokbuf.at[c, xy], tokbuf.at[c, xy], g2s.at[d], g2r.at[d], (t, peer_xy(d) * 2 + c))
        for d in range(1, n_xy)
    ]
    for copy in second:
        copy.start()
    third = [remote(tokbuf.at[c, xy], tokbuf.at[c, xy], g3s.at[0], g3r.at[0], sibling)]
    third[0].start()
    for d in range(1, n_xy):
        came = lax.rem(xy + n_xy - d, n_xy)
        remote(tokbuf.at[c, came], tokbuf.at[c, came], g2s.at[d], g2r.at[d], sibling).wait_recv()
        third.append(remote(tokbuf.at[c, came], tokbuf.at[c, came], g3s.at[d], g3r.at[d], sibling))
        third[-1].start()

    for copy in weights:
        copy.wait()
    shape = (tokens, group)
    place = lax.broadcasted_iota(jnp.int32, shape, 0)
    lane = lax.broadcasted_iota(jnp.int32, shape, 1)
    block = place // group
    unit_of = lax.rem(block, n_xy) * 2 + block // n_xy
    inner = lax.rem(place, group)
    token = ((inner // rows) * n_unit + unit_of) * rows + lax.rem(inner, rows)
    picked = jnp.zeros(shape, F32)
    for s in range(n_unit):
        picked = picked + jnp.where(token == lane + s * group, wbuf[s], 0.0)
    wcol[...] = jnp.broadcast_to(jnp.sum(picked, 1, keepdims=True), wcol.shape)

    for copy in second:
        copy.wait_send()
    for copy in third:
        copy.wait()
    for core in range(2):
        for p in range(0, n_xy, 2):
            parts = []
            for q in (p, p + 1):
                both = tokbuf[core, q].astype(F32)
                parts.append(jnp.concatenate([both[:group], both[group:]], 1))
            x_v[pl.ds((core * n_xy + p) * group, 2 * group), :] = jnp.concatenate(parts, 0).astype(BF16)

    dims = (((1,), (1,)), ((), ()))

    def hidden(i, _):
        spot = pl.ds(pl.multiple_of(i * unit_w, unit_w), unit_w)
        pltpu.make_async_copy(tg.at[0, pl.ds(0, unit_w)], gate_v.at[spot], gsem.at[i]).wait()
        pltpu.make_async_copy(tu.at[0, pl.ds(0, unit_w)], up_v.at[spot], usem.at[i]).wait()
        x = x_v[...]
        g = lax.dot_general(x, gate_v[spot, :], dims, preferred_element_type=F32)
        v = lax.dot_general(x, up_v[spot, :], dims, preferred_element_type=F32)
        scale = jnp.where(i < n_base, 1.0, wcol[:, :1])
        hid[i] = (jax.nn.silu(g) * v * scale).astype(BF16)
        return 0

    lax.fori_loop(0, n_hid, hidden, 0)

    for j in range(kept, n_col):
        for copy in down_copies(j):
            copy.start()

    pending = []

    def stage_a(j):
        for copy in down_copies(j):
            copy.wait()
        weight = down_v.at[j] if j < kept else gate_v.at[:, pl.ds((j - kept) * COLS, COLS)]
        if unit_w % 128 == 0:
            h = jnp.concatenate([hid[i] for i in range(n_hid)], 1)
            total = jnp.dot(h, weight[...], preferred_element_type=F32)
        else:
            total = jnp.zeros((tokens, COLS), F32)
            for i in range(n_hid):
                total += jnp.dot(hid[i], weight[pl.ds(i * unit_w, unit_w), :], preferred_element_type=F32)
        part[j] = total.reshape(2, n_xy, group, COLS)
        send_a[j] = part[j, 1 - c].reshape(half, COLS).astype(BF16)
        copy = remote(send_a.at[j], recv_a.at[j], as_.at[j], ar.at[j], sibling)
        copy.start()
        pending.append(copy)

    def stage_b(j):
        remote(send_a.at[j], recv_a.at[j], as_.at[j], ar.at[j], sibling).wait_recv()
        part[j, c] += recv_a[j].astype(F32).reshape(n_xy, group, COLS)
        for d in range(1, n_xy):
            block = part[j, c, peer_xy(d)]
            send_b[j, d] = jnp.concatenate([block[:, : COLS // 2], block[:, COLS // 2 :]], 0).astype(BF16)
            copy = remote(send_b.at[j, d], recv_b.at[j, d], bs.at[j, d], br.at[j, d], (t, peer_xy(d) * 2 + c))
            copy.start()
            pending.append(copy)

    def stage_c(j):
        total = part[j, c, xy]
        for d in range(1, n_xy):
            remote(send_b.at[j, d], recv_b.at[j, d], bs.at[j, d], br.at[j, d], sibling).wait_recv()
            both = recv_b[j, d].astype(F32)
            total = total + jnp.concatenate([both[:group], both[group:]], 1)
        for s in range(n_task):
            piece = total[s * rows : (s + 1) * rows]
            own_c[j, s] = piece
            send_c[j, s] = piece.astype(BF16)
        for d in range(1, n_task):
            to = lax.rem(t + d, n_task)
            copy = remote(send_c.at[j, to], recv_c.at[j, d], cs.at[j, d], cr.at[j, d], (to, u))
            copy.start()
            pending.append(copy)

    def stage_d(j):
        total = own_c[j, t]
        for d in range(1, n_task):
            remote(send_c.at[j, 0], recv_c.at[j, d], cs.at[j, d], cr.at[j, d], sibling).wait_recv()
            total = total + recv_c[j, d].astype(F32)
        out_ref[:, pl.ds(j * COLS, COLS)] = total.astype(BF16)

    for step in range(n_col + 3):
        for lag, stage in enumerate((stage_a, stage_b, stage_c, stage_d)):
            if 0 <= step - lag < n_col:
                stage(step - lag)
    for copy in pending:
        copy.wait_send()


def body(n_task, n_unit, tokens, router, bg, bu, bd, tg, tu, td):
    rows, d_model = tokens.shape
    group = n_task * rows
    total = group * n_unit
    n_xy = n_unit // 2
    base_w, task_w = bg.shape[0], tg.shape[1]
    unit_w = min(256, math.gcd(base_w, task_w))
    width = base_w + task_w
    n_hid = width // unit_w
    n_col = d_model // COLS
    half = total // 2
    vmem = pl.BlockSpec(memory_space=pltpu.VMEM)
    hbm = pl.BlockSpec(memory_space=pl.ANY)
    dma = pltpu.SemaphoreType.DMA
    return pl.pallas_call(
        functools.partial(kernel, n_task, n_unit),
        out_shape=jax.ShapeDtypeStruct((rows, d_model), BF16),
        in_specs=[vmem, vmem] + [hbm] * 6,
        out_specs=vmem,
        scratch_shapes=[
            pltpu.VMEM((width, d_model), BF16),
            pltpu.VMEM((width, d_model), BF16),
            pltpu.VMEM((n_col - REUSE, width, COLS), BF16),
            pltpu.VMEM((n_hid, total, unit_w), BF16),
            pltpu.VMEM((total, d_model), BF16),
            pltpu.VMEM((2, n_xy, 2 * group, d_model // 2), BF16),
            pltpu.VMEM((n_task, rows, d_model), BF16),
            pltpu.VMEM((group, d_model), F32),
            pltpu.VMEM((n_unit, 1, group), F32),
            pltpu.VMEM((total, 128), F32),
            pltpu.VMEM((n_col, 2, n_xy, group, COLS), F32),
            pltpu.VMEM((n_col, half, COLS), BF16),
            pltpu.VMEM((n_col, half, COLS), BF16),
            pltpu.VMEM((n_col, n_xy, 2 * group, COLS // 2), BF16),
            pltpu.VMEM((n_col, n_xy, 2 * group, COLS // 2), BF16),
            pltpu.VMEM((n_col, n_task, rows, COLS), BF16),
            pltpu.VMEM((n_col, n_task, rows, COLS), BF16),
            pltpu.VMEM((n_col, n_task, rows, COLS), F32),
            dma((n_hid,)), dma((n_hid,)), dma((n_col, 2)),
            dma((n_task,)), dma((n_task,)),
            dma((n_xy,)), dma((n_xy,)), dma((n_xy,)), dma((n_xy,)),
            dma((n_unit,)), dma((n_unit,)),
            dma((n_col,)), dma((n_col,)),
            dma((n_col, n_xy)), dma((n_col, n_xy)),
            dma((n_col, n_task)), dma((n_col, n_task)),
        ],
        compiler_params=pltpu.CompilerParams(
            collective_id=0, has_side_effects=True, vmem_limit_bytes=VMEM_LIMIT
        ),
        cost_estimate=pl.CostEstimate(
            flops=6 * total * width * d_model,
            bytes_accessed=6 * width * d_model,
            transcendentals=total * width,
        ),
        name="router_mixture",
    )(tokens, router.reshape(1, group), bg, bu, bd, tg, tu, td)


VMEM_LIMIT = 64 * 1024 * 1024


def solution(mesh):
    in_specs = (
        P(("task", "unit"), None),
        P("unit", "task"),
        P(("task", "unit"), None),
        P(("task", "unit"), None),
        P(("task", "unit"), None),
        P("task", "unit", None),
        P("task", "unit", None),
        P("task", "unit", None),
    )
    out_specs = P(("task", "unit"), None)
    part_fn = functools.partial(body, mesh.shape["task"], mesh.shape["unit"])
    return jax.shard_map(part_fn, mesh=mesh, in_specs=in_specs, out_specs=out_specs, check_vma=False)
```

time: 143 us -> 56.7 us (0.40)
  blocking collectives: 106 us -> 0 us
  Pallas kernels: 0 us -> 55.1 us
  matrix products: 34.9 us -> 0 us
    unnamed x2 -> x0, blocking collectives: 60.5 us -> none
    pallas_call x0 -> x1, Pallas kernels: none -> 55.1 us  [body(): pl.pallas_call(functools.partial(kernel, n_task, n_unit), out_shape=jax.S...]
    all_gather x1 -> x0, blocking collectives: 45 us -> none  [body(): piece = lax.all_gather(tokens, ('task', 'unit'), axis=0, tiled=True)]
    dot_general x4 -> x0, matrix products: 34.9 us -> none  [the longest x1 14.7 us: body(): jnp.dot(hidden[:, base_width:], own_down, preferred_element_type=jnp.floa...]
where the time goes in v1:
time: 56.7 us; the launch traced here: 56.4 us
  Pallas kernels  55.1 us (97%)
  local copies, waits for them, and re-layouts  1.34 us (2%)
    pallas_call x1, Pallas kernels, body(): pl.pallas_call(functools.partial(kernel, n_task, n_unit), out_shape=jax.S...  55.1 us
    unnamed x1, local copies, waits for them, and re-layouts  1.34 us

profile of v1, /device:TPU:0, one launch (start us, length us, event | category | flops | bytes accessed | tf_op | source)
XLA Modules:
  0.0 56.4 jit_solution(4802572784526933975)
XLA Ops:
  0.0 55.1 %router_mixture.1 = bf16[2,4096]{1,0:T(2,128)(2,1)} custom-call(bf16[2,4096]{1,0:T(2,128)(2,1)} %tok_ref.1, f32[1,8]{1,0:T(1,128)} %bitcast.1, bf16[512,4096]{1,0:T(8,128)(2,1)} %bg.1, bf16[512,4096]{1,0:T(8,128)(2,1)} %bu.1, bf16[512,4096]{1,0:T(8,128)(2,1)} %bd.1, bf16[1,2048,4096]{2,1,0:T(8,128)(2,1)} %tg.1, bf16[1,2048,4096]{2,1,0:T(8,128)(2,1)} %tu.1, ...), custom_call_target="tpu_custom_call" | custom-call | flops 4026531840 | bytes 62914560 | tf_op jit(solution)/shard_map/router_mixture/pallas_call | solution.py:235
  55.1 1.3 %copy.10 = bf16[2,4096]{1,0:T(2,128)(2,1)} copy(bf16[2,4096]{1,0:T(2,128)(2,1)} %router_mixture.1) | data formatting | bytes 32768

commit v2 on v1

--- a/solution.py
+++ b/solution.py
@@ -11,7 +11,8 @@
 MESH = pl.DeviceIdType.MESH
 F32 = jnp.float32
 BF16 = jnp.bfloat16
-COLS = 512
+COLS = 1024
+LAG = 4
 REUSE = 1
 
 
@@ -210,8 +211,8 @@
             total = total + recv_c[j, d].astype(F32)
         out_ref[:, pl.ds(j * COLS, COLS)] = total.astype(BF16)
 
-    for step in range(n_col + 3):
-        for lag, stage in enumerate((stage_a, stage_b, stage_c, stage_d)):
+    for step in range(n_col + 3 * LAG):
+        for lag, stage in ((0, stage_a), (LAG, stage_b), (2 * LAG, stage_c), (3 * LAG, stage_d)):
             if 0 <= step - lag < n_col:
                 stage(step - lag)
     for copy in pending:
@@ -224,7 +225,7 @@
     total = group * n_unit
     n_xy = n_unit // 2
     base_w, task_w = bg.shape[0], tg.shape[1]
-    unit_w = min(256, math.gcd(base_w, task_w))
+    unit_w = min(512, math.gcd(base_w, task_w))
     width = base_w + task_w
     n_hid = width // unit_w
     n_col = d_model // COLS

time: 56.7 us -> 45.2 us (0.80)
  Pallas kernels: 55.1 us -> 43.5 us
    pallas_call x1, Pallas kernels: 55.1 us -> 43.5 us  [body(): pl.pallas_call(functools.partial(kernel, n_task, n_unit), out_shape=jax.S...]
where the time goes in v2:
time: 45.2 us; the launch traced here: 44.8 us
  Pallas kernels  43.5 us (96%)
  local copies, waits for them, and re-layouts  1.34 us (3%)
    pallas_call x1, Pallas kernels, body(): pl.pallas_call(functools.partial(kernel, n_task, n_unit), out_shape=jax.S...  43.5 us
    unnamed x1, local copies, waits for them, and re-layouts  1.34 us

profile of v2, /device:TPU:0, one launch (start us, length us, event | category | flops | bytes accessed | tf_op | source)
XLA Modules:
  0.0 44.8 jit_solution(17248730325343291781)
XLA Ops:
  0.0 43.5 %router_mixture.1 = bf16[2,4096]{1,0:T(2,128)(2,1)} custom-call(bf16[2,4096]{1,0:T(2,128)(2,1)} %tok_ref.1, f32[1,8]{1,0:T(1,128)} %bitcast.1, bf16[512,4096]{1,0:T(8,128)(2,1)} %bg.1, bf16[512,4096]{1,0:T(8,128)(2,1)} %bu.1, bf16[512,4096]{1,0:T(8,128)(2,1)} %bd.1, bf16[1,2048,4096]{2,1,0:T(8,128)(2,1)} %tg.1, bf16[1,2048,4096]{2,1,0:T(8,128)(2,1)} %tu.1, ...), custom_call_target="tpu_custom_call" | custom-call | flops 4026531840 | bytes 62914560 | tf_op jit(solution)/shard_map/router_mixture/pallas_call | solution.py:236
  43.5 1.3 %copy.10 = bf16[2,4096]{1,0:T(2,128)(2,1)} copy(bf16[2,4096]{1,0:T(2,128)(2,1)} %router_mixture.1) | data formatting | bytes 32768

commit v3 on v2

--- a/solution.py
+++ b/solution.py
@@ -38,6 +38,12 @@
     n_col = d_model // COLS
     kept = n_col - REUSE
 
+    barrier = pltpu.get_barrier_semaphore()
+    for d in range(1, n_task):
+        pl.semaphore_signal(barrier, inc=1, device_id=(lax.rem(t + d, n_task), u), device_id_type=MESH)
+    for d in range(1, n_unit):
+        pl.semaphore_signal(barrier, inc=1, device_id=(t, lax.rem(u + d, n_unit)), device_id_type=MESH)
+
     for i in range(n_hid):
         for base, task, buf, sem in ((bg, tg, gate_v, gsem), (bu, tu, up_v, usem)):
             if i < n_base:
@@ -58,15 +64,6 @@
             pltpu.make_async_copy(td.at[0, :, cols], hi, dsem.at[j, 1]),
         )
 
-    for j in range(kept):
-        for copy in down_copies(j):
-            copy.start()
-
-    barrier = pltpu.get_barrier_semaphore()
-    for d in range(1, n_task):
-        pl.semaphore_signal(barrier, inc=1, device_id=(lax.rem(t + d, n_task), u), device_id_type=MESH)
-    for d in range(1, n_unit):
-        pl.semaphore_signal(barrier, inc=1, device_id=(t, lax.rem(u + d, n_unit)), device_id_type=MESH)
     pl.semaphore_wait(barrier, n_task + n_unit - 2)
 
     def remote(src, dst, ssem, rsem, dev):
@@ -113,6 +110,10 @@
         remote(tokbuf.at[c, came], tokbuf.at[c, came], g2s.at[d], g2r.at[d], sibling).wait_recv()
         third.append(remote(tokbuf.at[c, came], tokbuf.at[c, came], g3s.at[d], g3r.at[d], sibling))
         third[-1].start()
+
+    for j in range(kept):
+        for copy in down_copies(j):
+            copy.start()
 
     for copy in weights:
         copy.wait()

time: 45.2 us -> 45.2 us (level)
  no operation moved by 1% of the time
where the time goes in v3:
time: 45.2 us; the launch traced here: 44.8 us
  Pallas kernels  43.5 us (96%)
  local copies, waits for them, and re-layouts  1.34 us (3%)
    pallas_call x1, Pallas kernels, body(): pl.pallas_call(functools.partial(kernel, n_task, n_unit), out_shape=jax.S...  43.5 us
    unnamed x1, local copies, waits for them, and re-layouts  1.34 us

profile of v3, /device:TPU:0, one launch (start us, length us, event | category | flops | bytes accessed | tf_op | source)
XLA Modules:
  0.0 44.8 jit_solution(2219987862990314473)
XLA Ops:
  0.0 43.5 %router_mixture.1 = bf16[2,4096]{1,0:T(2,128)(2,1)} custom-call(bf16[2,4096]{1,0:T(2,128)(2,1)} %tok_ref.1, f32[1,8]{1,0:T(1,128)} %bitcast.1, bf16[512,4096]{1,0:T(8,128)(2,1)} %bg.1, bf16[512,4096]{1,0:T(8,128)(2,1)} %bu.1, bf16[512,4096]{1,0:T(8,128)(2,1)} %bd.1, bf16[1,2048,4096]{2,1,0:T(8,128)(2,1)} %tg.1, bf16[1,2048,4096]{2,1,0:T(8,128)(2,1)} %tu.1, ...), custom_call_target="tpu_custom_call" | custom-call | flops 4026531840 | bytes 62914560 | tf_op jit(solution)/shard_map/router_mixture/pallas_call | solution.py:237
  43.5 1.3 %copy.10 = bf16[2,4096]{1,0:T(2,128)(2,1)} copy(bf16[2,4096]{1,0:T(2,128)(2,1)} %router_mixture.1) | data formatting | bytes 32768
